TPU v7x, 512 devices: a whole 4x8x8 slice. The times are simulated.
512 devices in a mesh: img: 16 (over y, core), proj: 32 (over z, x).
Axes of the slice: x: 4, y: 8, z: 8, core: 2. Of those that a mesh axis runs over, the one named last changes fastest.
Arguments:
- images: bfloat16 [2048, 4096], P('img'), may hold values from -48 to 48
- projections: bfloat16 [2560, 4096], P('proj'), may hold values from -6 to 6
- noise_weight: float32 [4096], replicated, may hold values from 0.02 to 0.08
- defocus: float32 [2048], P('img'), may hold values from 2 to 8
- orient_count: int32 [2048], P('img'), may hold values from 160 to 2560, as said below
- term_limit: int32 [2048], P('img'), may hold values from 2048 to 4096
- block_plan: int32 [64], replicated, may hold values from 0 to 63, each once
Outputs:
- reconstruction: bfloat16 [2560, 4096], P('proj', 'img')
- evidence_next: float32 [2048], P('img')
Inputs may be any that keep to these rules, and one draw needn't show every extreme that they name: Orientations 0 to orient_count[i] - 1 are the significant ones of image i; some image has all 2560.
All inputs are finite; a program needn't handle non-finite values.
Results may differ from a plain program's by a relative error of at most 0.018.
Values may be sent and summed in bfloat16 or wider, within the bound.
No kernel may reach another device: no remote copies, remote signals or barrier semaphores. Data moves between devices by JAX's collectives and lax.ppermute only.
A program may use at most 64 MiB of HBM per device.

v0:
```python
import math
import jax
import jax.numpy as jnp
from jax import lax
from jax.sharding import PartitionSpec as P

F = 4096
BLOCK = 32


def sent_to_all(array, axis):
    peers = lax.axis_size(axis)
    return lax.all_to_all(
        jnp.broadcast_to(array[None], (peers, *array.shape)), axis, 0, 0, tiled=True
    )


def gathered_once(array, axis):
    leaves = jax.tree.leaves(array)
    turns = sorted(range(len(leaves)), key=lambda k: -leaves[k].size)
    width = (1, *leaves[turns[0]].shape)[-1]
    lines = [
        jnp.pad(leaves[k].reshape(-1), (0, -leaves[k].size % width)).reshape(-1, width)
        for k in turns
    ]
    both, at, found = (sent_to_all(jnp.concatenate(lines), axis), 0, {})
    for k, line in zip(turns, lines):
        slab = both[:, at : at + len(line)].reshape(len(both), -1)
        found[k] = slab[:, : leaves[k].size].reshape(-1, *leaves[k].shape)
        at += len(line)
    numbers = iter(range(len(leaves)))
    return jax.tree.map(lambda _: found[next(numbers)], array)


def combined_pairwise(pieces, combine):
    while len(jax.tree.leaves(pieces)[0]) > 1:
        pieces = jax.vmap(combine)(
            *(jax.tree.map(lambda part: part[side::2], pieces) for side in (0, 1))
        )
    return jax.tree.map(lambda part: part[0], pieces)


def joined_all(array, axis, combine):
    pieces = gathered_once(array, axis)
    return combined_pairwise(pieces, combine)


def cut_along(array, dim, peers):
    before, after = (array.shape[:dim], array.shape[dim + 1 :])
    return jnp.moveaxis(array.reshape(*before, peers, -1, *after), dim, 0)


def sum_at_owner(array, axis, dim):
    peers = lax.axis_size(axis)
    blocks = lax.all_to_all(cut_along(array, dim, peers), axis, 0, 0, tiled=True)
    return jnp.sum(blocks.astype(jnp.float32), axis=0)


def side_by_side(arrays, axis, dim, along):
    widths = [a.shape[along] for a in arrays]
    both = jnp.concatenate(arrays, axis=along)
    filled = sum_at_owner(both, axis, dim)
    return tuple(jnp.split(filled, [sum(widths[:k]) for k in range(1, len(widths))], axis=along))


def contrast_table(defocus, width):
    frequency = (jnp.arange(width, dtype=jnp.float32) + 1.0) / width
    return jnp.sin(2.0 * math.pi * defocus[:, None] * frequency[None, :] + 0.1)


def image_terms(pixels, noise_weight, defocus, limits):
    width = pixels.shape[1]
    contrast = contrast_table(defocus, width)
    keep_mask = (jnp.arange(width, dtype=jnp.int32)[None, :] < limits[:, None]).astype(jnp.float32)
    values = pixels.astype(jnp.float32)
    weighted = (keep_mask * noise_weight[None, :] * contrast * values).astype(jnp.bfloat16)
    weighted_sq = (keep_mask * noise_weight[None, :] * contrast * contrast).astype(jnp.bfloat16)
    back_images = (keep_mask * contrast * values).astype(jnp.bfloat16)
    return (weighted, weighted_sq, back_images)


def join_mass(first, second):
    joined = jnp.maximum(first[0], second[0])
    total = first[1] * jnp.exp(first[0] - joined) + second[1] * jnp.exp(second[0] - joined)
    return (joined, total)


def shards(images, projections, noise_weight, defocus, orient_count, term_limit, block_plan):
    proj_rows = projections.shape[0]
    img_rows = images.shape[0]
    weighted, weighted_sq, back_images = image_terms(images, noise_weight, defocus, term_limit)
    proj_sq = (projections.astype(jnp.float32) * projections.astype(jnp.float32)).astype(
        jnp.bfloat16
    )
    contract = (((1,), (1,)), ((), ()))
    scores = lax.dot_general(projections, weighted, contract, preferred_element_type=jnp.float32)
    scores = scores - 0.5 * lax.dot_general(
        proj_sq, weighted_sq, contract, preferred_element_type=jnp.float32
    )
    orient_ids = lax.axis_index("proj") * proj_rows + jnp.arange(proj_rows, dtype=jnp.int32)
    significant = orient_ids[:, None] < orient_count[None, :]
    local_peak = jnp.max(jnp.where(significant, scores, -1e30), axis=0)
    safe = jnp.where(significant, scores, local_peak[None, :])
    local_mass = jnp.sum(jnp.where(significant, jnp.exp(safe - local_peak[None, :]), 0.0), axis=0)
    row_peak, row_mass = joined_all((local_peak, local_mass), "proj", join_mass)
    log_evidence = row_peak + jnp.log(row_mass)
    posterior = jnp.where(significant, jnp.exp(scores - log_evidence[None, :]), 0.0).astype(
        jnp.bfloat16
    )
    contrast = contrast_table(defocus, F)
    keep_mask = (jnp.arange(F, dtype=jnp.int32)[None, :] < term_limit[:, None]).astype(jnp.float32)
    back_weights = (keep_mask * contrast * contrast).astype(jnp.bfloat16)
    part_images = jnp.dot(posterior, back_images, preferred_element_type=jnp.float32)
    part_weights = jnp.dot(posterior, back_weights, preferred_element_type=jnp.float32)
    sum_images, sum_weights = side_by_side(
        (part_images.astype(jnp.bfloat16), part_weights.astype(jnp.bfloat16)), "img", 1, 0
    )
    reconstruction = (sum_images / (sum_weights + 1.0)).astype(jnp.bfloat16)
    every_evidence = lax.all_gather(log_evidence, "img", axis=0, tiled=True)
    blocks = every_evidence.reshape(-1, BLOCK)
    local_blocks = img_rows // BLOCK
    slot_ids = lax.axis_index("img") * local_blocks + jnp.arange(local_blocks, dtype=jnp.int32)
    selector = (block_plan[None, :] == slot_ids[:, None]).astype(jnp.float32)
    own_blocks = jnp.dot(selector, blocks, precision=lax.Precision.HIGHEST)
    return (reconstruction, own_blocks.reshape(img_rows))


def solution(mesh):
    placed = (P("img", None), P("proj", None), P(), P("img"), P("img"), P("img"), P())
    return jax.shard_map(
        shards, mesh=mesh, in_specs=placed, out_specs=(P("proj", "img"), P("img")), check_vma=False
    )
```

profile of v0, /device:TPU:1, one launch (start us, length us, event | category | flops | bytes accessed | tf_op | source)
XLA Modules:
  0.0 112.6 jit_solution(15977206153363226754)
XLA Ops:
  0.7 0.7 broadcast_multiply_fusion
  1.3 0.0 copy-start
  1.3 0.0 copy-start.2
  1.3 0.0 copy-start.3
  1.3 0.0 copy-start.4
  1.3 9.5 %convolution_bitcast_fusion = f32[80,128]{1,0:T(8,128)S(1)} fusion(bf16[80,4096]{1,0:T(8,128)(2,1)} %param.8, bf16[128,4096]{1,0:T(8,128)(2,1)} %param.7, f32[4096]{0:T(1024)S(1)} %add_multiply_fusion, f32[128]{0:T(128)S(1)} %broadcast_multiply_fusion, f32[4096]{0:T(1024)} %param.9, s32[128]{0:T(128)} %param.12), kind=kOutput, calls=%fused_computation.18 | convolution fusion | flops 88080384 | bytes 1778688 | tf_op jit(solution)/shard_map/dot_general | solution.py:96
  10.8 0.0 copy-done
  10.8 0.0 copy-done.2
  10.9 0.0 copy-done.3
  10.9 0.0 copy-done.4
  10.9 7.8 %fusion.30 = (f32[128]{0:T(128)S(1)}, f32[80,128]{1,0:T(8,128)S(1)}) fusion(s32[128]{0:T(128)S(1)} %copy-done, s32[80]{0:T(128)S(1)} %iota_add_fusion.1, f32[80,128]{1,0:T(8,128)S(1)} %convolution_bitcast_fusion, f32[4096]{0:T(1024)S(1)} %add_multiply_fusion, f32[128]{0:T(128)S(1)} %broadcast_multiply_fusion, f32[4096]{0:T(1024)S(1)} %copy-done.3, ...), kind=kOutput, calls=%fused_computation.46 | convolution fusion | flops 88590208 | bytes 772416 | tf_op jit(solution)/shard_map/dot_general | solution.py:97
  18.7 0.1 fusion.33
  18.9 22.2 %all_to_all.10 = f32[32,2,128]{2,1,0:T(2,128)S(1)} all-to-all(f32[32,2,128]{2,1,0:T(2,128)S(1)} %broadcast_in_dim.21), channel_id=1, replica_groups=mesh['img'=16,'proj'=32] {'proj'}, dimensions={0} | all-to-all | bytes 65536 | tf_op jit(solution)/shard_map/all_to_all | solution.py:13
  41.5 0.0 copy-start.1
  41.5 7.4 %convolution_convert_fusion = bf16[80,4096]{1,0:T(8,128)(2,1)S(1)} fusion(f32[4096]{0:T(1024)S(1)} %add_multiply_fusion, f32[128]{0:T(128)S(1)} %broadcast_multiply_fusion, s32[128]{0:T(128)S(1)} %copy-done.4, f32[80,128]{1,0:T(8,128)S(1)} %get-tuple-element.13, f32[128]{0:T(128)S(1)} %bitcast.25, s32[128]{0:T(128)S(1)} %copy-done, s32[80]{0:T(128)S(1)} %iota_add_fusion.1), kind=kOutput, calls=%fused_computation | convolution fusion | flops 87400448 | bytes 715072 | tf_op jit(solution)/shard_map/dot_general | solution.py:114
  48.9 0.0 copy-done.1
  48.9 7.8 %convolution_convert_fusion.1 = bf16[80,4096]{1,0:T(8,128)(2,1)S(1)} fusion(bf16[128,4096]{1,0:T(8,128)(2,1)S(1)} %copy-done.1, f32[4096]{0:T(1024)S(1)} %add_multiply_fusion, f32[128]{0:T(128)S(1)} %broadcast_multiply_fusion, s32[128]{0:T(128)S(1)} %copy-done.4, f32[80,128]{1,0:T(8,128)S(1)} %get-tuple-element.13, f32[128]{0:T(128)S(1)} %bitcast.26, ...), kind=kOutput, calls=%fused_computation.1 | convolution fusion | flops 87924736 | bytes 1763648 | tf_op jit(solution)/shard_map/dot_general | solution.py:113
  56.7 0.1 pad_maximum_fusion
  56.8 1.2 %copy.14 = bf16[20,16,8,256]{3,2,0,1:T(8,128)(2,1)} copy(bf16[20,16,8,256]{3,2,1,0:T(8,128)(2,1)S(1)} %bitcast.18) | data formatting | bytes 2621440 | tf_op jit(solution)/shard_map/reshape | solution.py:50
  58.0 0.0 copy-start.5
  58.0 9.3 %all-to-all-start.1 = ((bf16[16,160,256]{2,1,0:T(8,128)(2,1)}), bf16[16,160,256]{2,1,0:T(8,128)(2,1)S(1)}, u32[]{:S(2)}, u32[]{:S(2)}) async-start(bf16[16,160,256]{2,1,0:T(8,128)(2,1)} %bitcast.17), calls=%async_computation.1 | async-start | bytes 2621440 | tf_op jit(solution)/shard_map/all_to_all | solution.py:55
  67.4 42.3 %all-gather = f32[1,2048]{1,0:T(1,128)S(1)} all-gather(f32[1,128]{1,0:T(1,128)S(1)} %log_add_fusion), channel_id=2, replica_groups=mesh['img'=16,'proj'=32] {'img'}, dimensions={1}, use_global_device_ids=true | all-gather | bytes 8704 | tf_op jit(solution)/shard_map/all_gather | solution.py:119
  109.7 0.5 broadcast.80
  110.2 0.7 reduce.3
  110.9 0.1 reshape.53
  110.9 0.0 copy-done.5
  110.9 0.2 fusion.35
  111.1 0.6 reshape.54
  111.7 0.0 all-to-all-done.1
  111.7 0.2 convert_reduce_fusion
  111.9 0.6 fusion.29
  (27 shorter events, 0.4 us)
Async XLA Ops:
  1.3 9.5 %copy-start = (s32[128]{0:T(128)S(1)}, s32[128]{0:T(128)}, u32[]{:S(2)}) copy-start(s32[128]{0:T(128)} %param.11) | copy-start | bytes 1540
  1.3 9.5 %copy-start.2 = (bf16[80,4096]{1,0:T(8,128)(2,1)S(1)}, bf16[80,4096]{1,0:T(8,128)(2,1)}, u32[]{:S(2)}) copy-start(bf16[80,4096]{1,0:T(8,128)(2,1)} %param.8) | copy-start | bytes 1966084
  1.3 9.5 %copy-start.3 = (f32[4096]{0:T(1024)S(1)}, f32[4096]{0:T(1024)}, u32[]{:S(2)}) copy-start(f32[4096]{0:T(1024)} %param.9) | copy-start | bytes 49156
  1.3 9.5 %copy-start.4 = (s32[128]{0:T(128)S(1)}, s32[128]{0:T(128)}, u32[]{:S(2)}) copy-start(s32[128]{0:T(128)} %param.12) | copy-start | bytes 1540
  41.5 7.5 %copy-start.1 = (bf16[128,4096]{1,0:T(8,128)(2,1)S(1)}, bf16[128,4096]{1,0:T(8,128)(2,1)}, u32[]{:S(2)}) copy-start(bf16[128,4096]{1,0:T(8,128)(2,1)} %param.7) | copy-start | bytes 3145732
  58.0 52.9 %copy-start.5 = (s32[64]{0:T(128)S(1)}, s32[64]{0:T(128)}, u32[]{:S(2)}) copy-start(s32[64]{0:T(128)} %param.13) | copy-start | bytes 772
  58.0 53.7 %all-to-all-start.1 = ((bf16[16,160,256]{2,1,0:T(8,128)(2,1)}), bf16[16,160,256]{2,1,0:T(8,128)(2,1)S(1)}, u32[]{:S(2)}, u32[]{:S(2)}) async-start(bf16[16,160,256]{2,1,0:T(8,128)(2,1)} %bitcast.17), calls=%async_computation.1 | async-start | bytes 2621440 | tf_op jit(solution)/shard_map/all_to_all | solution.py:55
where the time goes:
time: 113 us
  blocking collectives  64.5 us (57%)
  matrix products  32.7 us (29%)
  starting transfers between devices  9.35 us (8%)
  local copies, waits for them, and re-layouts  2.71 us (2%)
  other arithmetic  2.46 us (2%)
    all_gather x1, blocking collectives, shards(): every_evidence = lax.all_gather(log_evidence, 'img', axis=0, tiled=True)  42.3 us
    all_to_all x1, blocking collectives, sent_to_all(): lax.all_to_all(jnp.broadcast_to(array[None], (peers, *array.shape)), axis...  22.2 us
    dot_general x1, matrix products, shards(): lax.dot_general(projections, weighted, contract, preferred_element_type=j...  9.5 us
    all_to_all x1, starting transfers between devices, sum_at_owner(): lax.all_to_all(cut_along(array, dim, peers), axis, 0, 0, tiled=True)  9.35 us
    dot_general x1, matrix products, shards(): lax.dot_general(proj_sq, weighted_sq, contract, preferred_element_type=jn...  7.83 us
    dot_general x1, matrix products, shards(): jnp.dot(posterior, back_images, preferred_element_type=jnp.float32)  7.77 us
    dot_general x1, matrix products, shards(): jnp.dot(posterior, back_weights, preferred_element_type=jnp.float32)  7.44 us
  transfers between devices with their start and end apart: 1, of which 0 were waited for; matrix products, arithmetic and copies ran while one was open for 2% of the time, Pallas kernels for 0%

commit v1 on v0

--- a/solution.py
+++ b/solution.py
@@ -6,6 +6,19 @@
 
 F = 4096
 BLOCK = 32
+
+
+def gather_around(x, axis, dim):
+    ways = lax.axis_size(axis)
+    up = [(d, (d + 1) % ways) for d in range(ways)]
+    down = [(d, (d - 1) % ways) for d in range(ways)]
+    earlier, later = ([x], [x])
+    for _ in range(ways // 2):
+        earlier.append(lax.ppermute(earlier[-1], axis, up))
+    for _ in range((ways - 1) // 2):
+        later.append(lax.ppermute(later[-1], axis, down))
+    line = jnp.concatenate([*earlier[::-1], *later[1:]], axis=dim)
+    return jnp.roll(line, (lax.axis_index(axis) - ways // 2) * x.shape[dim], axis=dim)
 
 
 def sent_to_all(array, axis):
@@ -116,7 +129,7 @@
         (part_images.astype(jnp.bfloat16), part_weights.astype(jnp.bfloat16)), "img", 1, 0
     )
     reconstruction = (sum_images / (sum_weights + 1.0)).astype(jnp.bfloat16)
-    every_evidence = lax.all_gather(log_evidence, "img", axis=0, tiled=True)
+    every_evidence = gather_around(log_evidence, "img", 0)
     blocks = every_evidence.reshape(-1, BLOCK)
     local_blocks = img_rows // BLOCK
     slot_ids = lax.axis_index("img") * local_blocks + jnp.arange(local_blocks, dtype=jnp.int32)

time: 113 us -> 129 us (1.14)
  blocking collectives: 64.5 us -> 22.2 us
  waiting for transfers between devices: 0.01 us -> 35 us
  starting transfers between devices: 9.35 us -> 33.3 us
    all_gather x1 -> x0, blocking collectives: 42.3 us -> none  [shards(): every_evidence = lax.all_gather(log_evidence, 'img', axis=0, tiled=True)]
    ppermute x0 -> x15, waiting for transfers between devices: none -> 34 us  [the longest x7 31 us: gather_around(): later.append(lax.ppermute(later[-1], axis, down))]
    ppermute x0 -> x15, starting transfers between devices: none -> 22.8 us  [the longest x7 13.9 us: gather_around(): later.append(lax.ppermute(later[-1], axis, down))]
  transfers between devices with their start and end apart: 1 -> 16, of which waited for: 0 -> 8; matrix products, arithmetic and copies ran while one was open for 2% -> 14% of each run, Pallas kernels for 0% -> 0%
where the time goes in v1:
time: 129 us
  waiting for transfers between devices  35 us (27%)
  starting transfers between devices  33.3 us (26%)
  matrix products  32.7 us (25%)
  blocking collectives  22.2 us (17%)
  local copies, waits for them, and re-layouts  2.51 us (2%)
  other arithmetic  1.8 us (1%)
    ppermute x7, waiting for transfers between devices, gather_around(): later.append(lax.ppermute(later[-1], axis, down))  31 us
    all_to_all x1, blocking collectives, sent_to_all(): lax.all_to_all(jnp.broadcast_to(array[None], (peers, *array.shape)), axis...  22.2 us
    ppermute x7, starting transfers between devices, gather_around(): later.append(lax.ppermute(later[-1], axis, down))  13.9 us
    all_to_all x1, starting transfers between devices, sum_at_owner(): lax.all_to_all(cut_along(array, dim, peers), axis, 0, 0, tiled=True)  10.5 us
    dot_general x1, matrix products, shards(): lax.dot_general(projections, weighted, contract, preferred_element_type=j...  9.5 us
    ppermute x8, starting transfers between devices, gather_around(): earlier.append(lax.ppermute(earlier[-1], axis, up))  8.91 us
    dot_general x1, matrix products, shards(): lax.dot_general(proj_sq, weighted_sq, contract, preferred_element_type=jn...  7.83 us
    dot_general x1, matrix products, shards(): jnp.dot(posterior, back_weights, preferred_element_type=jnp.float32)  7.66 us
  transfers between devices with their start and end apart: 16, of which 8 were waited for; matrix products, arithmetic and copies ran while one was open for 14% of the time, Pallas kernels for 0%

profile of v1, /device:TPU:1, one launch (start us, length us, event | category | flops | bytes accessed | tf_op | source)
XLA Modules:
  0.0 128.6 jit_solution(2312195611295535635)
XLA Ops:
  0.7 0.7 broadcast_multiply_fusion
  1.3 9.5 %convolution_bitcast_fusion = f32[80,128]{1,0:T(8,128)S(1)} fusion(bf16[80,4096]{1,0:T(8,128)(2,1)} %param.8, bf16[128,4096]{1,0:T(8,128)(2,1)} %param.7, f32[4096]{0:T(1024)S(1)} %add_multiply_fusion, f32[128]{0:T(128)S(1)} %broadcast_multiply_fusion, f32[4096]{0:T(1024)} %param.9, s32[128]{0:T(128)} %param.12), kind=kOutput, calls=%fused_computation.18 | convolution fusion | flops 88080384 | bytes 1778688 | tf_op jit(solution)/shard_map/dot_general | solution.py:109
  10.9 7.8 %fusion.30 = (f32[128]{0:T(128)S(1)}, f32[80,128]{1,0:T(8,128)S(1)}) fusion(s32[128]{0:T(128)S(1)} %copy-done, s32[80]{0:T(128)S(1)} %iota_add_fusion.1, f32[80,128]{1,0:T(8,128)S(1)} %convolution_bitcast_fusion, f32[4096]{0:T(1024)S(1)} %add_multiply_fusion, f32[128]{0:T(128)S(1)} %broadcast_multiply_fusion, f32[4096]{0:T(1024)S(1)} %copy-done.3, ...), kind=kOutput, calls=%fused_computation.46 | convolution fusion | flops 88590208 | bytes 772416 | tf_op jit(solution)/shard_map/dot_general | solution.py:110
  18.7 0.1 fusion.33
  18.9 22.2 %all_to_all.10 = f32[32,2,128]{2,1,0:T(2,128)S(1)} all-to-all(f32[32,2,128]{2,1,0:T(2,128)S(1)} %broadcast_in_dim.21), channel_id=1, replica_groups=mesh['img'=16,'proj'=32] {'proj'}, dimensions={0} | all-to-all | bytes 65536 | tf_op jit(solution)/shard_map/all_to_all | solution.py:26
  41.5 3.3 %collective-permute-start = (f32[128]{0:T(128)S(1)}, f32[128]{0:T(128)S(1)}, u32[]{:S(2)}, u32[]{:S(2)}) collective-permute-start(f32[128]{0:T(128)S(1)} %add_bitcast_fusion), channel_id=1, source_target_pairs={{0,32},{32,64},{64,96},{96,128},{128,160},{160,192},{192,224},{224... | collective-permute-start | bytes 1544 | tf_op jit(solution)/shard_map/ppermute | solution.py:17
  44.8 0.7 collective-permute-done
  45.5 2.2 %collective-permute-start.1 = (f32[128]{0:T(128)S(1)}, f32[128]{0:T(128)S(1)}, u32[]{:S(2)}, u32[]{:S(2)}) collective-permute-start(f32[128]{0:T(128)S(1)} %collective-permute-done), channel_id=1, source_target_pairs={{0,32},{32,64},{64,96},{96,128},{128,160},{160,192},{192,224},{224... | collective-permute-start | bytes 1544 | tf_op jit(solution)/shard_map/ppermute | solution.py:17
  47.8 0.7 collective-permute-done.1
  48.5 2.2 %collective-permute-start.2 = (f32[128]{0:T(128)S(1)}, f32[128]{0:T(128)S(1)}, u32[]{:S(2)}, u32[]{:S(2)}) collective-permute-start(f32[128]{0:T(128)S(1)} %collective-permute-done.1), channel_id=1, source_target_pairs={{0,32},{32,64},{64,96},{96,128},{128,160},{160,192},{192,224},{224... | collective-permute-start | bytes 1544 | tf_op jit(solution)/shard_map/ppermute | solution.py:17
  50.7 1.3 %collective-permute-start.9 = (f32[128]{0:T(128)S(1)}, f32[128]{0:T(128)S(1)}, u32[]{:S(2)}, u32[]{:S(2)}) collective-permute-start(f32[128]{0:T(128)S(1)} %collective-permute-done.8), channel_id=1, source_target_pairs={{0,480},{32,0},{64,32},{96,64},{128,96},{160,128},{192,160},{224,1... | collective-permute-start | bytes 1544 | tf_op jit(solution)/shard_map/ppermute | solution.py:19
  52.0 0.5 collective-permute-done.2
  52.6 1.1 collective-permute-start.3
  53.7 2.5 %collective-permute-start.10 = (f32[128]{0:T(128)S(1)}, f32[128]{0:T(128)S(1)}, u32[]{:S(2)}, u32[]{:S(2)}) collective-permute-start(f32[128]{0:T(128)S(1)} %collective-permute-done.9), channel_id=1, source_target_pairs={{0,480},{32,0},{64,32},{96,64},{128,96},{160,128},{192,160},{224,1... | collective-permute-start | bytes 1544 | tf_op jit(solution)/shard_map/ppermute | solution.py:19
  56.2 0.5 collective-permute-done.3
  56.7 0.3 collective-permute-done.10
  57.0 3.4 %collective-permute-start.11 = (f32[128]{0:T(128)S(1)}, f32[128]{0:T(128)S(1)}, u32[]{:S(2)}, u32[]{:S(2)}) collective-permute-start(f32[128]{0:T(128)S(1)} %collective-permute-done.10), channel_id=1, source_target_pairs={{0,480},{32,0},{64,32},{96,64},{128,96},{160,128},{192,160},{224,1... | collective-permute-start | bytes 1544 | tf_op jit(solution)/shard_map/ppermute | solution.py:19
  60.4 0.5 collective-permute-done.4
  60.9 7.6 %convolution_convert_fusion.1 = bf16[80,4096]{1,0:T(8,128)(2,1)S(1)} fusion(bf16[128,4096]{1,0:T(8,128)(2,1)S(1)} %copy-done.1, f32[4096]{0:T(1024)S(1)} %add_multiply_fusion, f32[128]{0:T(128)S(1)} %broadcast_multiply_fusion, s32[128]{0:T(128)S(1)} %copy-done.4, f32[80,128]{1,0:T(8,128)S(1)} %get-tuple-element.13, f32[128]{0:T(128)S(1)} %add_bitcast_fusion, ...), kind=kOutput, calls=%fused_computation.1 | convolution fusion | flops 87924736 | bytes 1763648 | tf_op jit(solution)/shard_map/dot_general | solution.py:126
  68.5 3.6 %collective-permute-start.12 = (f32[128]{0:T(128)S(1)}, f32[128]{0:T(128)S(1)}, u32[]{:S(2)}, u32[]{:S(2)}) collective-permute-start(f32[128]{0:T(128)S(1)} %collective-permute-done.11), channel_id=1, source_target_pairs={{0,480},{32,0},{64,32},{96,64},{128,96},{160,128},{192,160},{224,1... | collective-permute-start | bytes 1544 | tf_op jit(solution)/shard_map/ppermute | solution.py:19
  72.1 7.7 %convolution_convert_fusion = bf16[80,4096]{1,0:T(8,128)(2,1)S(1)} fusion(f32[4096]{0:T(1024)S(1)} %add_multiply_fusion, f32[128]{0:T(128)S(1)} %broadcast_multiply_fusion, s32[128]{0:T(128)S(1)} %copy-done.4, f32[80,128]{1,0:T(8,128)S(1)} %get-tuple-element.13, f32[128]{0:T(128)S(1)} %add_bitcast_fusion, s32[128]{0:T(128)S(1)} %copy-done, ...), kind=kOutput, calls=%fused_computation | convolution fusion | flops 87400448 | bytes 715072 | tf_op jit(solution)/shard_map/dot_general | solution.py:127
  79.8 3.0 %collective-permute-start.13 = (f32[128]{0:T(128)S(1)}, f32[128]{0:T(128)S(1)}, u32[]{:S(2)}, u32[]{:S(2)}) collective-permute-start(f32[128]{0:T(128)S(1)} %collective-permute-done.12), channel_id=1, source_target_pairs={{0,480},{32,0},{64,32},{96,64},{128,96},{160,128},{192,160},{224,1... | collective-permute-start | bytes 1544 | tf_op jit(solution)/shard_map/ppermute | solution.py:19
  82.7 0.1 pad_maximum_fusion
  82.8 1.2 copy.14
  84.1 10.5 %all-to-all-start.1 = ((bf16[16,160,256]{2,1,0:T(8,128)(2,1)}), bf16[16,160,256]{2,1,0:T(8,128)(2,1)S(1)}, u32[]{:S(2)}, u32[]{:S(2)}) async-start(bf16[16,160,256]{2,1,0:T(8,128)(2,1)} %bitcast.18), calls=%async_computation.1 | async-start | bytes 2621440 | tf_op jit(solution)/shard_map/all_to_all | solution.py:68
  94.6 0.1 collective-permute-start.14
  94.9 30.7 %collective-permute-done.14 = f32[128]{0:T(128)S(1)} collective-permute-done((f32[128]{0:T(128)S(1)}, f32[128]{0:T(128)S(1)}, u32[]{:S(2)}, u32[]{:S(2)}) %collective-permute-start.14) | collective-permute-done | bytes 544 | tf_op jit(solution)/shard_map/ppermute | solution.py:19
  125.9 0.2 fusion.35
  126.1 0.6 reshape.54
  126.7 1.0 all-to-all-done.1
  127.7 0.2 convert_reduce_fusion
  127.9 0.6 fusion.29
  (87 shorter events, 0.8 us)
Async XLA Ops:
  1.3 9.5 %copy-start = (s32[128]{0:T(128)S(1)}, s32[128]{0:T(128)}, u32[]{:S(2)}) copy-start(s32[128]{0:T(128)} %param.11) | copy-start | bytes 1540
  1.3 9.5 %copy-start.2 = (bf16[80,4096]{1,0:T(8,128)(2,1)S(1)}, bf16[80,4096]{1,0:T(8,128)(2,1)}, u32[]{:S(2)}) copy-start(bf16[80,4096]{1,0:T(8,128)(2,1)} %param.8) | copy-start | bytes 1966084
  1.3 9.5 %copy-start.3 = (f32[4096]{0:T(1024)S(1)}, f32[4096]{0:T(1024)}, u32[]{:S(2)}) copy-start(f32[4096]{0:T(1024)} %param.9) | copy-start | bytes 49156
  1.3 9.5 %copy-start.4 = (s32[128]{0:T(128)S(1)}, s32[128]{0:T(128)}, u32[]{:S(2)}) copy-start(s32[128]{0:T(128)} %param.12) | copy-start | bytes 1540
  10.9 50.0 %copy-start.1 = (bf16[128,4096]{1,0:T(8,128)(2,1)S(1)}, bf16[128,4096]{1,0:T(8,128)(2,1)}, u32[]{:S(2)}) copy-start(bf16[128,4096]{1,0:T(8,128)(2,1)} %param.7) | copy-start | bytes 3145732
  41.5 4.0 %collective-permute-start = (f32[128]{0:T(128)S(1)}, f32[128]{0:T(128)S(1)}, u32[]{:S(2)}, u32[]{:S(2)}) collective-permute-start(f32[128]{0:T(128)S(1)} %add_bitcast_fusion), channel_id=1, source_target_pairs={{0,32},{32,64},{64,96},{96,128},{128,160},{160,192},{192,224},{224... | collective-permute-start | bytes 1544 | tf_op jit(solution)/shard_map/ppermute | solution.py:17
  45.5 3.0 %collective-permute-start.1 = (f32[128]{0:T(128)S(1)}, f32[128]{0:T(128)S(1)}, u32[]{:S(2)}, u32[]{:S(2)}) collective-permute-start(f32[128]{0:T(128)S(1)} %collective-permute-done), channel_id=1, source_target_pairs={{0,32},{32,64},{64,96},{96,128},{128,160},{160,192},{192,224},{224... | collective-permute-start | bytes 1544 | tf_op jit(solution)/shard_map/ppermute | solution.py:17
  47.7 3.0 %collective-permute-start.8 = (f32[128]{0:T(128)S(1)}, f32[128]{0:T(128)S(1)}, u32[]{:S(2)}, u32[]{:S(2)}) collective-permute-start(f32[128]{0:T(128)S(1)} %add_bitcast_fusion), channel_id=1, source_target_pairs={{0,480},{32,0},{64,32},{96,64},{128,96},{160,128},{192,160},{224,1... | collective-permute-start | bytes 1544 | tf_op jit(solution)/shard_map/ppermute | solution.py:19
  48.5 4.1 %collective-permute-start.2 = (f32[128]{0:T(128)S(1)}, f32[128]{0:T(128)S(1)}, u32[]{:S(2)}, u32[]{:S(2)}) collective-permute-start(f32[128]{0:T(128)S(1)} %collective-permute-done.1), channel_id=1, source_target_pairs={{0,32},{32,64},{64,96},{96,128},{128,160},{160,192},{192,224},{224... | collective-permute-start | bytes 1544 | tf_op jit(solution)/shard_map/ppermute | solution.py:17
  50.7 3.0 %collective-permute-start.9 = (f32[128]{0:T(128)S(1)}, f32[128]{0:T(128)S(1)}, u32[]{:S(2)}, u32[]{:S(2)}) collective-permute-start(f32[128]{0:T(128)S(1)} %collective-permute-done.8), channel_id=1, source_target_pairs={{0,480},{32,0},{64,32},{96,64},{128,96},{160,128},{192,160},{224,1... | collective-permute-start | bytes 1544 | tf_op jit(solution)/shard_map/ppermute | solution.py:19
  52.6 4.2 %collective-permute-start.3 = (f32[128]{0:T(128)S(1)}, f32[128]{0:T(128)S(1)}, u32[]{:S(2)}, u32[]{:S(2)}) collective-permute-start(f32[128]{0:T(128)S(1)} %collective-permute-done.2), channel_id=1, source_target_pairs={{0,32},{32,64},{64,96},{96,128},{128,160},{160,192},{192,224},{224... | collective-permute-start | bytes 1544 | tf_op jit(solution)/shard_map/ppermute | solution.py:17
  53.7 3.3 %collective-permute-start.10 = (f32[128]{0:T(128)S(1)}, f32[128]{0:T(128)S(1)}, u32[]{:S(2)}, u32[]{:S(2)}) collective-permute-start(f32[128]{0:T(128)S(1)} %collective-permute-done.9), channel_id=1, source_target_pairs={{0,480},{32,0},{64,32},{96,64},{128,96},{160,128},{192,160},{224,1... | collective-permute-start | bytes 1544 | tf_op jit(solution)/shard_map/ppermute | solution.py:19
  56.7 4.2 %collective-permute-start.4 = (f32[128]{0:T(128)S(1)}, f32[128]{0:T(128)S(1)}, u32[]{:S(2)}, u32[]{:S(2)}) collective-permute-start(f32[128]{0:T(128)S(1)} %collective-permute-done.3), channel_id=1, source_target_pairs={{0,32},{32,64},{64,96},{96,128},{128,160},{160,192},{192,224},{224... | collective-permute-start | bytes 1544 | tf_op jit(solution)/shard_map/ppermute | solution.py:17
  57.0 11.5 %collective-permute-start.11 = (f32[128]{0:T(128)S(1)}, f32[128]{0:T(128)S(1)}, u32[]{:S(2)}, u32[]{:S(2)}) collective-permute-start(f32[128]{0:T(128)S(1)} %collective-permute-done.10), channel_id=1, source_target_pairs={{0,480},{32,0},{64,32},{96,64},{128,96},{160,128},{192,160},{224,1... | collective-permute-start | bytes 1544 | tf_op jit(solution)/shard_map/ppermute | solution.py:19
  60.9 11.2 %collective-permute-start.5 = (f32[128]{0:T(128)S(1)}, f32[128]{0:T(128)S(1)}, u32[]{:S(2)}, u32[]{:S(2)}) collective-permute-start(f32[128]{0:T(128)S(1)} %collective-permute-done.4), channel_id=1, source_target_pairs={{0,32},{32,64},{64,96},{96,128},{128,160},{160,192},{192,224},{224... | collective-permute-start | bytes 1544 | tf_op jit(solution)/shard_map/ppermute | solution.py:17
  68.5 11.3 %collective-permute-start.12 = (f32[128]{0:T(128)S(1)}, f32[128]{0:T(128)S(1)}, u32[]{:S(2)}, u32[]{:S(2)}) collective-permute-start(f32[128]{0:T(128)S(1)} %collective-permute-done.11), channel_id=1, source_target_pairs={{0,480},{32,0},{64,32},{96,64},{128,96},{160,128},{192,160},{224,1... | collective-permute-start | bytes 1544 | tf_op jit(solution)/shard_map/ppermute | solution.py:19
  72.1 10.6 %collective-permute-start.6 = (f32[128]{0:T(128)S(1)}, f32[128]{0:T(128)S(1)}, u32[]{:S(2)}, u32[]{:S(2)}) collective-permute-start(f32[128]{0:T(128)S(1)} %collective-permute-done.5), channel_id=1, source_target_pairs={{0,32},{32,64},{64,96},{96,128},{128,160},{160,192},{192,224},{224... | collective-permute-start | bytes 1544 | tf_op jit(solution)/shard_map/ppermute | solution.py:17
  79.8 14.8 %collective-permute-start.13 = (f32[128]{0:T(128)S(1)}, f32[128]{0:T(128)S(1)}, u32[]{:S(2)}, u32[]{:S(2)}) collective-permute-start(f32[128]{0:T(128)S(1)} %collective-permute-done.12), channel_id=1, source_target_pairs={{0,480},{32,0},{64,32},{96,64},{128,96},{160,128},{192,160},{224,1... | collective-permute-start | bytes 1544 | tf_op jit(solution)/shard_map/ppermute | solution.py:19
  82.7 12.0 %collective-permute-start.7 = (f32[128]{0:T(128)S(1)}, f32[128]{0:T(128)S(1)}, u32[]{:S(2)}, u32[]{:S(2)}) collective-permute-start(f32[128]{0:T(128)S(1)} %collective-permute-done.6), channel_id=1, source_target_pairs={{0,32},{32,64},{64,96},{96,128},{128,160},{160,192},{192,224},{224... | collective-permute-start | bytes 1544 | tf_op jit(solution)/shard_map/ppermute | solution.py:17
  84.1 41.9 %copy-start.5 = (s32[64]{0:T(128)S(1)}, s32[64]{0:T(128)}, u32[]{:S(2)}) copy-start(s32[64]{0:T(128)} %param.13) | copy-start | bytes 772
  84.1 43.7 %all-to-all-start.1 = ((bf16[16,160,256]{2,1,0:T(8,128)(2,1)}), bf16[16,160,256]{2,1,0:T(8,128)(2,1)S(1)}, u32[]{:S(2)}, u32[]{:S(2)}) async-start(bf16[16,160,256]{2,1,0:T(8,128)(2,1)} %bitcast.18), calls=%async_computation.1 | async-start | bytes 2621440 | tf_op jit(solution)/shard_map/all_to_all | solution.py:68
  94.6 31.0 %collective-permute-start.14 = (f32[128]{0:T(128)S(1)}, f32[128]{0:T(128)S(1)}, u32[]{:S(2)}, u32[]{:S(2)}) collective-permute-start(f32[128]{0:T(128)S(1)} %collective-permute-done.13), channel_id=1, source_target_pairs={{0,480},{32,0},{64,32},{96,64},{128,96},{160,128},{192,160},{224,1... | collective-permute-start | bytes 1544 | tf_op jit(solution)/shard_map/ppermute | solution.py:19
